TPU v7x, 32 devices: a whole 2x2x4 slice. The times are simulated.
32 devices in a mesh: frame: 8 (over z, y), audio: 4 (over x, core).
Axes of the slice: x: 2, y: 2, z: 4, core: 2. Of those that a mesh axis runs over, the one named last changes fastest.
Arguments:
- video: bfloat16 [25088, 768], P(('frame', 'audio')), may hold values from -6 to 6
- audio: bfloat16 [8192, 768], P(('frame', 'audio')), may hold values from -6 to 6
- w_query: bfloat16 [768, 768], replicated, may hold values from -9 to 9
- w_key: bfloat16 [768, 768], replicated, may hold values from -0.21875 to 0.21875
- w_value: bfloat16 [768, 768], replicated, may hold values from -0.21875 to 0.21875
- w_out: bfloat16 [768, 768], replicated, may hold values from -0.21875 to 0.21875
- grad_output: bfloat16 [25088, 768], P(('frame', 'audio')), may hold values from -6 to 6
- intersection_tiles: int32 [128, 8], P(('frame', 'audio')), may hold values from 0 to 63, as said below
- intersection_count: int32 [128], P(('frame', 'audio')), may hold values from 1 to 8
- tile_fill: int32 [64], P(('frame', 'audio')), may hold values from 32 to 128
Outputs:
- output: bfloat16 [25088, 768], P(('frame', 'audio'))
- grad_video: bfloat16 [25088, 768], P(('frame', 'audio'))
- grad_audio: bfloat16 [8192, 768], P(('frame', 'audio'))
- grad_w_query: float32 [768, 768], replicated
- grad_w_key: float32 [768, 768], replicated
- grad_w_value: float32 [768, 768], replicated
- grad_w_out: float32 [768, 768], replicated
Inputs may be any that keep to these rules, and one draw needn't show every extreme that they name: `intersection_tiles`: entries j < intersection_count[f] of frame f are distinct tiles of index in [(f // 4 - 2) * 2, (f // 4 + 3) * 2); other entries are any tile.
All inputs are finite; a program needn't handle non-finite values.
Results may differ from a plain program's by a relative error of at most 0.0085.
The roundings to bfloat16 on the way count: a program that leaves them out, or rounds other values in their place, can miss the bound.
Values may be sent and summed in bfloat16 or wider, within the bound.
A program may use at most 192 MiB of HBM per device.

v0:
```python
import math

import jax
import jax.numpy as jnp
from jax import lax
from jax.sharding import PartitionSpec as P

HEADS = 12
TILE = 128
REACH = 2


def shifted(block, axis, distance):
    devices = range(lax.axis_size(axis))
    route = [(i - distance, i) for i in devices if i - distance in devices]
    return lax.ppermute(block, axis, route)


def normalize(row_block):
    centred = row_block.astype(jnp.float32)
    centred = centred - jnp.mean(centred, axis=-1, keepdims=True)
    inverse = lax.rsqrt(jnp.mean(centred * centred, axis=-1, keepdims=True) + 1e-05)
    normed_hat = centred * inverse
    return (normed_hat.astype(jnp.bfloat16), normed_hat, inverse)


def normalize_back(gradient, normed_hat, inverse):
    first = jnp.mean(gradient, axis=-1, keepdims=True)
    second = jnp.mean(gradient * normed_hat, axis=-1, keepdims=True)
    return inverse * (gradient - first - normed_hat * second)


def frame_step(
    query_frame, dcontext_frame, key_window, value_window, filled_window, local_tile, used_count
):
    features = query_frame.shape[1]
    head_size = features // HEADS
    score_scale = 1.0 / math.sqrt(head_size)
    chosen_keys = key_window[local_tile].reshape(-1, HEADS, head_size)
    chosen_values = value_window[local_tile].reshape(-1, HEADS, head_size)
    listed = (jnp.arange(local_tile.shape[0]) < used_count).astype(jnp.float32)
    visible = (filled_window[local_tile] * listed[:, None]).reshape(-1)
    queries = query_frame.reshape(-1, HEADS, head_size)
    dcontext = dcontext_frame.reshape(-1, HEADS, head_size)
    scores = (
        jnp.einsum("phd,khd->hpk", queries, chosen_keys, preferred_element_type=jnp.float32)
        * score_scale
    )
    scores = jnp.where(visible > 0, scores, -1e30)
    highest = jnp.max(scores, axis=-1, keepdims=True)
    exponent = jnp.exp(scores - highest) * visible
    attention = exponent / jnp.sum(exponent, axis=-1, keepdims=True)
    attention_low = attention.astype(jnp.bfloat16)
    context = jnp.einsum(
        "hpk,khd->phd", attention_low, chosen_values, preferred_element_type=jnp.float32
    )
    context = context.astype(jnp.bfloat16).reshape(-1, features)
    dattention = jnp.einsum(
        "phd,khd->hpk", dcontext, chosen_values, preferred_element_type=jnp.float32
    )
    dscores = (
        attention
        * (dattention - jnp.sum(attention * dattention, axis=-1, keepdims=True))
        * score_scale
    )
    dscores = dscores.astype(jnp.bfloat16)
    dquery = jnp.einsum("hpk,khd->phd", dscores, chosen_keys, preferred_element_type=jnp.float32)
    dquery = dquery.astype(jnp.bfloat16).reshape(-1, features)
    dkeys = jnp.einsum("hpk,phd->khd", dscores, queries, preferred_element_type=jnp.float32)
    dvalues = jnp.einsum(
        "hpk,phd->khd", attention_low, dcontext, preferred_element_type=jnp.float32
    )
    dkeys = dkeys.reshape(local_tile.shape[0], -1, features)
    dvalues = dvalues.reshape(local_tile.shape[0], -1, features)
    return (context, dquery, dkeys, dvalues)


def block_step(
    query_block, dcontext_block, key_window, value_window, filled_window, local_block, count_block
):
    empty = jnp.zeros(key_window.shape, jnp.float32)

    def per_frame(running, inputs_now):
        query_frame, dcontext_frame, local_tile, used_count = inputs_now
        context, dquery, dkeys, dvalues = frame_step(
            query_frame,
            dcontext_frame,
            key_window,
            value_window,
            filled_window,
            local_tile,
            used_count,
        )
        return (
            (running[0].at[local_tile].add(dkeys), running[1].at[local_tile].add(dvalues)),
            (context, dquery),
        )

    (summed_keys, summed_values), (context, dquery) = lax.scan(
        per_frame, (empty, empty), (query_block, dcontext_block, local_block, count_block)
    )
    return (context, dquery, summed_keys.astype(jnp.bfloat16), summed_values.astype(jnp.bfloat16))


def per_device(
    video,
    audio,
    w_query,
    w_key,
    w_value,
    w_out,
    grad_output,
    intersection_tiles,
    intersection_count,
    tile_fill,
):
    tiles_dev = tile_fill.shape[0]
    window_tiles = (2 * REACH + 1) * tiles_dev
    frames = intersection_count.shape[0]
    features = video.shape[1]
    contract_rows = (((0,), (0,)), ((), ()))
    contract_cols = (((1,), (1,)), ((), ()))
    video_normed, video_hat, video_inverse = normalize(video)
    audio_normed, audio_hat, audio_inverse = normalize(audio)
    query = jnp.dot(video_normed, w_query, preferred_element_type=jnp.float32).astype(jnp.bfloat16)
    dcontext = lax.dot_general(
        grad_output, w_out, contract_cols, preferred_element_type=jnp.float32
    ).astype(jnp.bfloat16)
    filled = (lax.broadcasted_iota(jnp.int32, (tiles_dev, TILE), 1) < tile_fill[:, None]).astype(
        jnp.bfloat16
    )
    device_index = lax.axis_index(("frame", "audio"))
    normed_tiles = audio_normed.reshape(tiles_dev, TILE, features)
    normed_parts, filled_parts = ([], [])
    for offset in range(-REACH, REACH + 1):
        if offset == 0:
            received = (normed_tiles, filled)
        else:
            received = shifted((normed_tiles, filled), ("frame", "audio"), -offset)
        normed_parts.append(received[0])
        filled_parts.append(received[1])
    normed_window = jnp.concatenate(normed_parts, axis=0).reshape(-1, features)
    key_window = (
        jnp.dot(normed_window, w_key, preferred_element_type=jnp.float32)
        .astype(jnp.bfloat16)
        .reshape(window_tiles, TILE, features)
    )
    value_window = (
        jnp.dot(normed_window, w_value, preferred_element_type=jnp.float32)
        .astype(jnp.bfloat16)
        .reshape(window_tiles, TILE, features)
    )
    filled_window = jnp.concatenate(filled_parts, axis=0).astype(jnp.float32)
    local_block = jnp.clip(
        intersection_tiles - (device_index - REACH) * tiles_dev, 0, window_tiles - 1
    )
    context, dquery, dkeys, dvalues = block_step(
        query.reshape(frames, -1, features),
        dcontext.reshape(frames, -1, features),
        key_window,
        value_window,
        filled_window,
        local_block,
        intersection_count,
    )
    context = context.reshape(-1, features)
    dquery = dquery.reshape(-1, features)
    attended = jnp.dot(context, w_out, preferred_element_type=jnp.float32)
    output = (video.astype(jnp.float32) + attended).astype(jnp.bfloat16)
    grad_out_part = lax.dot_general(
        context, grad_output, contract_rows, preferred_element_type=jnp.float32
    )
    grad_query_part = lax.dot_general(
        video_normed, dquery, contract_rows, preferred_element_type=jnp.float32
    )
    dvideo_normed = lax.dot_general(
        dquery, w_query, contract_cols, preferred_element_type=jnp.float32
    )
    grad_video = (
        grad_output.astype(jnp.float32) + normalize_back(dvideo_normed, video_hat, video_inverse)
    ).astype(jnp.bfloat16)
    own_first = REACH * tiles_dev
    dkeys_flat = dkeys.reshape(-1, features)
    dvalues_flat = dvalues.reshape(-1, features)
    dnormed_window = lax.dot_general(
        dkeys_flat, w_key, contract_cols, preferred_element_type=jnp.float32
    )
    dnormed_window = dnormed_window + lax.dot_general(
        dvalues_flat, w_value, contract_cols, preferred_element_type=jnp.float32
    )
    dnormed_window = dnormed_window.reshape(window_tiles, TILE, features)
    grad_key_part = lax.dot_general(
        normed_window, dkeys_flat, contract_rows, preferred_element_type=jnp.float32
    )
    grad_value_part = lax.dot_general(
        normed_window, dvalues_flat, contract_rows, preferred_element_type=jnp.float32
    )
    daudio_normed = dnormed_window[own_first : own_first + tiles_dev]
    for offset in range(-REACH, REACH + 1):
        if offset != 0:
            first_tile = (offset + REACH) * tiles_dev
            returned = shifted(
                dnormed_window[first_tile : first_tile + tiles_dev], ("frame", "audio"), offset
            )
            daudio_normed = daudio_normed + returned
    daudio_normed = daudio_normed.reshape(-1, features)
    grad_audio = normalize_back(daudio_normed, audio_hat, audio_inverse).astype(jnp.bfloat16)
    summed = lax.psum(
        (grad_query_part, grad_key_part, grad_value_part, grad_out_part), ("frame", "audio")
    )
    return (output, grad_video, grad_audio, summed[0], summed[1], summed[2], summed[3])


def solution(mesh):
    in_specs = (
        P(("frame", "audio"), None),
        P(("frame", "audio"), None),
        P(),
        P(),
        P(),
        P(),
        P(("frame", "audio"), None),
        P(("frame", "audio"), None),
        P(("frame", "audio")),
        P(("frame", "audio")),
    )
    out_specs = (
        P(("frame", "audio"), None),
        P(("frame", "audio"), None),
        P(("frame", "audio"), None),
        P(),
        P(),
        P(),
        P(),
    )
    return jax.shard_map(
        per_device, mesh=mesh, in_specs=in_specs, out_specs=out_specs, check_vma=False
    )
```

profile of v0, /device:TPU:0, one launch (start us, length us, event | category | flops | bytes accessed | tf_op | source)
XLA Modules:
  0.0 867.6 jit_solution(270577902120161424)
XLA Ops:
  44.3 10.5 %collective-permute-done.7 = bf16[2,128,768]{1,2,0:T(8,128)(2,1)} collective-permute-done((bf16[2,128,768]{1,2,0:T(8,128)(2,1)S(1)}, bf16[2,128,768]{1,2,0:T(8,128)(2,1)}, u32[]{:S(2)}, u32[]{:S(2)}) %collective-permute-start.7) | collective-permute-done | bytes 393248 | tf_op jit(solution)/shard_map/ppermute | solution.py:16
  71.1 536.1 %while.16 = (s32[]{:T(128)}, f32[10,128,768]{2,1,0:T(8,128)}, f32[10,128,768]{2,1,0:T(8,128)}, bf16[4,196,768]{2,1,0:T(8,128)(2,1)}, bf16[4,196,768]{2,1,0:T(8,1...) while((s32[]{:T(128)}, f32[10,128,768]{2,1,0:T(8,128)}, ...), condition=%wide.region_10.11_spmd, body=%wide.region_4.10_spmd.sunk | while | flops 1906967296 | bytes 166828368 | solution.py:99
  92.0 6.6 fusion.131
  98.6 9.5 %fusion.132 = (f32[12,196]{1,0:T(8,128)}, f32[12,196,1024]{2,1,0:T(8,128)}) fusion(f32[1024]{0:T(1024)S(1)} %copy-done.23, pred[1024]{0:T(1024)(128)(4,1)} %get-tuple-element.226, bf16[196,12,64]{0,2,1:T(8,128)(2,1)S(1)} %bitcast.136, bf16[1024,12,64]{0,2,1:T(8,128)(2,1)} %reshape.252), kind=kOutput, calls=%fused_computation.98.clone.1 | convolution fusion | flops 320324608 | bytes 11522240 | tf_op jit(solution)/shard_map/while/body/eval_jaxpr/sub | solution.py:51
  108.2 6.3 fusion.136
  114.4 25.7 %fusion.135 = bf16[12,64,196]{2,1,0:T(8,128)(2,1)S(1)} fusion(bf16[1024,12,64]{0,2,1:T(8,128)(2,1)} %reshape.252, f32[12,196,1024]{2,1,0:T(8,128)} %fusion.131, f32[12,196,1024]{2,1,0:T(8,128)} %get-tuple-element.227, f32[12,196]{1,0:T(8,128)} %get-tuple-element.228), kind=kOutput, calls=%fused_computation.24.clone.1 | convolution fusion | flops 325294400 | bytes 21150912 | tf_op jit(solution)/shard_map/while/body/eval_jaxpr/hpk,khd->phd/dot_general | solution.py:67
  140.2 27.2 %fusion.133 = f32[12,64,1024]{2,1,0:T(8,128)} fusion(bf16[196,12,64]{0,2,1:T(8,128)(2,1)S(1)} %bitcast.137, f32[12,196,1024]{2,1,0:T(8,128)} %fusion.131, f32[12,196,1024]{2,1,0:T(8,128)} %get-tuple-element.227, f32[12,196]{1,0:T(8,128)S(1)} %copy-done.40), kind=kOutput, calls=%fused_computation.18.clone.1 | convolution fusion | flops 325143872 | bytes 22723776 | tf_op jit(solution)/shard_map/while/body/eval_jaxpr/hpk,phd->khd/dot_general | solution.py:69
  186.4 7.8 scatter_fusion
  194.3 7.9 scatter_fusion.1
  223.7 6.6 fusion.131
  230.3 9.5 %fusion.132 = (f32[12,196]{1,0:T(8,128)}, f32[12,196,1024]{2,1,0:T(8,128)}) fusion(f32[1024]{0:T(1024)S(1)} %copy-done.23, pred[1024]{0:T(1024)(128)(4,1)} %get-tuple-element.226, bf16[196,12,64]{0,2,1:T(8,128)(2,1)S(1)} %bitcast.136, bf16[1024,12,64]{0,2,1:T(8,128)(2,1)} %reshape.252), kind=kOutput, calls=%fused_computation.98.clone.1 | convolution fusion | flops 320324608 | bytes 11522240 | tf_op jit(solution)/shard_map/while/body/eval_jaxpr/sub | solution.py:51
  239.8 6.3 fusion.136
  246.1 25.7 %fusion.135 = bf16[12,64,196]{2,1,0:T(8,128)(2,1)S(1)} fusion(bf16[1024,12,64]{0,2,1:T(8,128)(2,1)} %reshape.252, f32[12,196,1024]{2,1,0:T(8,128)} %fusion.131, f32[12,196,1024]{2,1,0:T(8,128)} %get-tuple-element.227, f32[12,196]{1,0:T(8,128)} %get-tuple-element.228), kind=kOutput, calls=%fused_computation.24.clone.1 | convolution fusion | flops 325294400 | bytes 21150912 | tf_op jit(solution)/shard_map/while/body/eval_jaxpr/hpk,khd->phd/dot_general | solution.py:67
  271.9 27.2 %fusion.133 = f32[12,64,1024]{2,1,0:T(8,128)} fusion(bf16[196,12,64]{0,2,1:T(8,128)(2,1)S(1)} %bitcast.137, f32[12,196,1024]{2,1,0:T(8,128)} %fusion.131, f32[12,196,1024]{2,1,0:T(8,128)} %get-tuple-element.227, f32[12,196]{1,0:T(8,128)S(1)} %copy-done.40), kind=kOutput, calls=%fused_computation.18.clone.1 | convolution fusion | flops 325143872 | bytes 22723776 | tf_op jit(solution)/shard_map/while/body/eval_jaxpr/hpk,phd->khd/dot_general | solution.py:69
  318.1 7.7 scatter_fusion
  325.9 7.7 scatter_fusion.1
  355.1 6.6 fusion.131
  361.7 9.5 %fusion.132 = (f32[12,196]{1,0:T(8,128)}, f32[12,196,1024]{2,1,0:T(8,128)}) fusion(f32[1024]{0:T(1024)S(1)} %copy-done.23, pred[1024]{0:T(1024)(128)(4,1)} %get-tuple-element.226, bf16[196,12,64]{0,2,1:T(8,128)(2,1)S(1)} %bitcast.136, bf16[1024,12,64]{0,2,1:T(8,128)(2,1)} %reshape.252), kind=kOutput, calls=%fused_computation.98.clone.1 | convolution fusion | flops 320324608 | bytes 11522240 | tf_op jit(solution)/shard_map/while/body/eval_jaxpr/sub | solution.py:51
  371.2 6.3 fusion.136
  377.5 25.7 %fusion.135 = bf16[12,64,196]{2,1,0:T(8,128)(2,1)S(1)} fusion(bf16[1024,12,64]{0,2,1:T(8,128)(2,1)} %reshape.252, f32[12,196,1024]{2,1,0:T(8,128)} %fusion.131, f32[12,196,1024]{2,1,0:T(8,128)} %get-tuple-element.227, f32[12,196]{1,0:T(8,128)} %get-tuple-element.228), kind=kOutput, calls=%fused_computation.24.clone.1 | convolution fusion | flops 325294400 | bytes 21150912 | tf_op jit(solution)/shard_map/while/body/eval_jaxpr/hpk,khd->phd/dot_general | solution.py:67
  403.3 27.2 %fusion.133 = f32[12,64,1024]{2,1,0:T(8,128)} fusion(bf16[196,12,64]{0,2,1:T(8,128)(2,1)S(1)} %bitcast.137, f32[12,196,1024]{2,1,0:T(8,128)} %fusion.131, f32[12,196,1024]{2,1,0:T(8,128)} %get-tuple-element.227, f32[12,196]{1,0:T(8,128)S(1)} %copy-done.40), kind=kOutput, calls=%fused_computation.18.clone.1 | convolution fusion | flops 325143872 | bytes 22723776 | tf_op jit(solution)/shard_map/while/body/eval_jaxpr/hpk,phd->khd/dot_general | solution.py:69
  449.5 7.9 scatter_fusion
  457.4 7.9 scatter_fusion.1
  486.7 6.6 fusion.131
  493.4 9.5 %fusion.132 = (f32[12,196]{1,0:T(8,128)}, f32[12,196,1024]{2,1,0:T(8,128)}) fusion(f32[1024]{0:T(1024)S(1)} %copy-done.23, pred[1024]{0:T(1024)(128)(4,1)} %get-tuple-element.226, bf16[196,12,64]{0,2,1:T(8,128)(2,1)S(1)} %bitcast.136, bf16[1024,12,64]{0,2,1:T(8,128)(2,1)} %reshape.252), kind=kOutput, calls=%fused_computation.98.clone.1 | convolution fusion | flops 320324608 | bytes 11522240 | tf_op jit(solution)/shard_map/while/body/eval_jaxpr/sub | solution.py:51
  502.9 6.3 fusion.136
  509.2 25.7 %fusion.135 = bf16[12,64,196]{2,1,0:T(8,128)(2,1)S(1)} fusion(bf16[1024,12,64]{0,2,1:T(8,128)(2,1)} %reshape.252, f32[12,196,1024]{2,1,0:T(8,128)} %fusion.131, f32[12,196,1024]{2,1,0:T(8,128)} %get-tuple-element.227, f32[12,196]{1,0:T(8,128)} %get-tuple-element.228), kind=kOutput, calls=%fused_computation.24.clone.1 | convolution fusion | flops 325294400 | bytes 21150912 | tf_op jit(solution)/shard_map/while/body/eval_jaxpr/hpk,khd->phd/dot_general | solution.py:67
  535.0 27.2 %fusion.133 = f32[12,64,1024]{2,1,0:T(8,128)} fusion(bf16[196,12,64]{0,2,1:T(8,128)(2,1)S(1)} %bitcast.137, f32[12,196,1024]{2,1,0:T(8,128)} %fusion.131, f32[12,196,1024]{2,1,0:T(8,128)} %get-tuple-element.227, f32[12,196]{1,0:T(8,128)S(1)} %copy-done.40), kind=kOutput, calls=%fused_computation.18.clone.1 | convolution fusion | flops 325143872 | bytes 22723776 | tf_op jit(solution)/shard_map/while/body/eval_jaxpr/hpk,phd->khd/dot_general | solution.py:69
  581.2 7.8 scatter_fusion
  589.0 7.9 scatter_fusion.1
  650.0 45.3 %collective-permute-done.11 = f32[2,128,768]{2,1,0:T(8,128)S(1)} collective-permute-done((f32[2,128,768]{2,1,0:T(8,128)S(1)}, f32[2,128,768]{2,1,0:T(8,128)S(1)}, u32[]{:S(2)}, u32[]{:S(2)}) %collective-permute-start.11) | collective-permute-done | bytes 786464 | tf_op jit(solution)/shard_map/ppermute | solution.py:16
  697.7 153.1 %all-reduce.3.cloned.1.call-done = (f32[768,768]{1,0:T(8,128)}, f32[768,768]{1,0:T(8,128)}, f32[768,768]{1,0:T(8,128)}, f32[768,768]{1,0:T(8,128)}) async-done(((f32[768,768]{1,0:T(8,128)}, f32[768,768]{1,0:T(8,128)}, f32[768,768]{1,0:T(8,128)}, f32[768,768]{1,0:T(8,128)}), (f32[768,768]{1,0:T(8,128)}, f32[768,768]{1,0:T(8,128)}, f32[768,768]{1,0:T(8,128)}, ...) | async-done | bytes 9437200 | tf_op jit(solution)/shard_map/psum | solution.py:208
  (292 shorter events, 269.3 us)
Async XLA Ops:
  7.2 56.3 %copy-start = (bf16[768,768]{1,0:T(8,128)(2,1)S(1)}, bf16[768,768]{1,0:T(8,128)(2,1)}, u32[]{:S(2)}) copy-start(bf16[768,768]{1,0:T(8,128)(2,1)} %param.15) | copy-start | bytes 3538948
  7.2 21.2 %copy-start.4 = (bf16[784,768]{1,0:T(8,128)(2,1)S(1)}, bf16[784,768]{1,0:T(8,128)(2,1)}, u32[]{:S(2)}) copy-start(bf16[784,768]{1,0:T(8,128)(2,1)} %param.12) | copy-start | bytes 3612676
  7.2 843.5 %all-reduce.3.cloned.1.call-start = ((), (), s32[]{:S(2)}) async-start(), calls=%async_computation | async-start | bytes 18874368 | tf_op jit(solution)/shard_map/psum | solution.py:208
  8.1 24.5 %collective-permute-start.3 = (bf16[2,128]{1,0:T(2,128)(2,1)S(1)}, bf16[2,128]{1,0:T(2,128)(2,1)S(1)}, u32[]{:S(2)}, u32[]{:S(2)}) collective-permute-start(bf16[2,128]{1,0:T(2,128)(2,1)S(1)} %compare_convert_fusion.1), channel_id=1, source_target_pairs={{2,0},{3,1},{4,2},{5,3},{6,4},{7,5},{8,6},{9,7},{10,8},{11,9},{12,... | collective-permute-start | bytes 1544 | tf_op jit(solution)/shard_map/ppermute | solution.py:16
  9.4 25.6 %collective-permute-start.2 = (bf16[2,128]{1,0:T(2,128)(2,1)S(1)}, bf16[2,128]{1,0:T(2,128)(2,1)S(1)}, u32[]{:S(2)}, u32[]{:S(2)}) collective-permute-start(bf16[2,128]{1,0:T(2,128)(2,1)S(1)} %compare_convert_fusion.1), channel_id=1, source_target_pairs={{1,0},{2,1},{3,2},{4,3},{5,4},{6,5},{7,6},{8,7},{9,8},{10,9},{11,1... | collective-permute-start | bytes 1544 | tf_op jit(solution)/shard_map/ppermute | solution.py:16
  10.7 29.1 %collective-permute-start.1 = (bf16[2,128]{1,0:T(2,128)(2,1)S(1)}, bf16[2,128]{1,0:T(2,128)(2,1)S(1)}, u32[]{:S(2)}, u32[]{:S(2)}) collective-permute-start(bf16[2,128]{1,0:T(2,128)(2,1)S(1)} %compare_convert_fusion.1), channel_id=1, source_target_pairs={{0,1},{1,2},{2,3},{3,4},{4,5},{5,6},{6,7},{7,8},{8,9},{9,10},{10,1... | collective-permute-start | bytes 1544 | tf_op jit(solution)/shard_map/ppermute | solution.py:16
  17.6 11.6 %copy-start.36 = (bf16[768,768]{1,0:T(8,128)(2,1)S(1)}, bf16[768,768]{1,0:T(8,128)(2,1)}, u32[]{:S(2)}) copy-start(bf16[768,768]{1,0:T(8,128)(2,1)} %param.14) | copy-start | bytes 3538948
  17.6 24.5 %collective-permute-start.5 = (bf16[2,128,768]{1,2,0:T(8,128)(2,1)S(1)}, bf16[2,128,768]{1,2,0:T(8,128)(2,1)}, u32[]{:S(2)}, u32[]{:S(2)}) collective-permute-start(bf16[2,128,768]{1,2,0:T(8,128)(2,1)S(1)} %copy.29), channel_id=1, source_target_pairs={{0,1},{1,2},{2,3},{3,4},{4,5},{5,6},{6,7},{7,8},{8,9},{9,10},{10,1... | collective-permute-start | bytes 1179656 | tf_op jit(solution)/shard_map/ppermute | solution.py:16
  23.6 17.5 %collective-permute-start.4 = (bf16[2,128,768]{1,2,0:T(8,128)(2,1)S(1)}, bf16[2,128,768]{1,2,0:T(8,128)(2,1)}, u32[]{:S(2)}, u32[]{:S(2)}) collective-permute-start(bf16[2,128,768]{1,2,0:T(8,128)(2,1)S(1)} %copy.29), channel_id=1, source_target_pairs={{0,2},{1,3},{2,4},{3,5},{4,6},{5,7},{6,8},{7,9},{8,10},{9,11},{10,... | collective-permute-start | bytes 1179656 | tf_op jit(solution)/shard_map/ppermute | solution.py:16
  32.6 8.4 collective-permute-start
  35.0 8.3 collective-permute-start.6
  39.8 15.1 %collective-permute-start.7 = (bf16[2,128,768]{1,2,0:T(8,128)(2,1)S(1)}, bf16[2,128,768]{1,2,0:T(8,128)(2,1)}, u32[]{:S(2)}, u32[]{:S(2)}) collective-permute-start(bf16[2,128,768]{1,2,0:T(8,128)(2,1)S(1)} %copy.29), channel_id=1, source_target_pairs={{2,0},{3,1},{4,2},{5,3},{6,4},{7,5},{8,6},{9,7},{10,8},{11,9},{12,... | collective-permute-start | bytes 1179656 | tf_op jit(solution)/shard_map/ppermute | solution.py:16
  92.0 6.6 copy-start.23
  98.6 9.5 %copy-start.1 = (bf16[1024,12,64]{0,2,1:T(8,128)(2,1)S(1)}, bf16[1024,12,64]{0,2,1:T(8,128)(2,1)}, u32[]{:S(2)}) copy-start(bf16[1024,12,64]{0,2,1:T(8,128)(2,1)} %reshape.251) | copy-start | bytes 4718596 | tf_op jit(solution)/shard_map/while
  114.4 25.7 %copy-start.40 = (f32[12,196]{1,0:T(8,128)S(1)}, f32[12,196]{1,0:T(8,128)}, u32[]{:S(2)}) copy-start(f32[12,196]{1,0:T(8,128)} %get-tuple-element.228) | copy-start | bytes 28228 | tf_op jit(solution)/shard_map/while
  194.3 8.8 %copy-start.34 = (s32[4,8]{1,0:T(4,128)S(1)}, s32[4,8]{1,0:T(4,128)}, u32[]{:S(2)}) copy-start(s32[4,8]{1,0:T(4,128)} %copy-done.33) | copy-start | bytes 388 | tf_op jit(solution)/shard_map/while
  230.3 9.5 %copy-start.1 = (bf16[1024,12,64]{0,2,1:T(8,128)(2,1)S(1)}, bf16[1024,12,64]{0,2,1:T(8,128)(2,1)}, u32[]{:S(2)}) copy-start(bf16[1024,12,64]{0,2,1:T(8,128)(2,1)} %reshape.251) | copy-start | bytes 4718596 | tf_op jit(solution)/shard_map/while
  246.1 25.7 %copy-start.40 = (f32[12,196]{1,0:T(8,128)S(1)}, f32[12,196]{1,0:T(8,128)}, u32[]{:S(2)}) copy-start(f32[12,196]{1,0:T(8,128)} %get-tuple-element.228) | copy-start | bytes 28228 | tf_op jit(solution)/shard_map/while
  325.8 8.6 copy-start.34
  361.7 9.5 %copy-start.1 = (bf16[1024,12,64]{0,2,1:T(8,128)(2,1)S(1)}, bf16[1024,12,64]{0,2,1:T(8,128)(2,1)}, u32[]{:S(2)}) copy-start(bf16[1024,12,64]{0,2,1:T(8,128)(2,1)} %reshape.251) | copy-start | bytes 4718596 | tf_op jit(solution)/shard_map/while
  377.5 25.7 %copy-start.40 = (f32[12,196]{1,0:T(8,128)S(1)}, f32[12,196]{1,0:T(8,128)}, u32[]{:S(2)}) copy-start(f32[12,196]{1,0:T(8,128)} %get-tuple-element.228) | copy-start | bytes 28228 | tf_op jit(solution)/shard_map/while
  457.4 8.7 %copy-start.34 = (s32[4,8]{1,0:T(4,128)S(1)}, s32[4,8]{1,0:T(4,128)}, u32[]{:S(2)}) copy-start(s32[4,8]{1,0:T(4,128)} %copy-done.33) | copy-start | bytes 388 | tf_op jit(solution)/shard_map/while
  493.4 9.5 %copy-start.1 = (bf16[1024,12,64]{0,2,1:T(8,128)(2,1)S(1)}, bf16[1024,12,64]{0,2,1:T(8,128)(2,1)}, u32[]{:S(2)}) copy-start(bf16[1024,12,64]{0,2,1:T(8,128)(2,1)} %reshape.251) | copy-start | bytes 4718596 | tf_op jit(solution)/shard_map/while
  509.2 25.7 %copy-start.40 = (f32[12,196]{1,0:T(8,128)S(1)}, f32[12,196]{1,0:T(8,128)}, u32[]{:S(2)}) copy-start(f32[12,196]{1,0:T(8,128)} %get-tuple-element.228) | copy-start | bytes 28228 | tf_op jit(solution)/shard_map/while
  589.0 8.8 %copy-start.34 = (s32[4,8]{1,0:T(4,128)S(1)}, s32[4,8]{1,0:T(4,128)}, u32[]{:S(2)}) copy-start(s32[4,8]{1,0:T(4,128)} %copy-done.33) | copy-start | bytes 388 | tf_op jit(solution)/shard_map/while
  615.6 7.2 copy-start.13
  634.3 10.3 %copy-start.20 = (bf16[784,768]{1,0:T(8,128)(2,1)S(1)}, bf16[784,768]{1,0:T(8,128)(2,1)}, u32[]{:S(2)}) copy-start(bf16[784,768]{1,0:T(8,128)(2,1)} %reshape.183) | copy-start | bytes 3612676
  634.3 10.3 %copy-start.37 = (bf16[768,768]{1,0:T(8,128)(2,1)S(1)}, bf16[768,768]{1,0:T(8,128)(2,1)}, u32[]{:S(2)}) copy-start(bf16[768,768]{1,0:T(8,128)(2,1)} %param.14) | copy-start | bytes 3538948
  634.7 60.6 %collective-permute-start.11 = (f32[2,128,768]{2,1,0:T(8,128)S(1)}, f32[2,128,768]{2,1,0:T(8,128)S(1)}, u32[]{:S(2)}, u32[]{:S(2)}) collective-permute-start(f32[2,128,768]{2,1,0:T(8,128)S(1)} %bitcast.149), channel_id=1, source_target_pairs={{0,2},{1,3},{2,4},{3,5},{4,6},{5,7},{6,8},{7,9},{8,10},{9,11},{10,... | collective-permute-start | bytes 2359304 | tf_op jit(solution)/shard_map/ppermute | solution.py:16
  640.5 54.8 %collective-permute-start.8 = (f32[2,128,768]{2,1,0:T(8,128)S(1)}, f32[2,128,768]{2,1,0:T(8,128)S(1)}, u32[]{:S(2)}, u32[]{:S(2)}) collective-permute-start(f32[2,128,768]{2,1,0:T(8,128)S(1)} %bitcast.148), channel_id=1, source_target_pairs={{2,0},{3,1},{4,2},{5,3},{6,4},{7,5},{8,6},{9,7},{10,8},{11,9},{12,... | collective-permute-start | bytes 2359304 | tf_op jit(solution)/shard_map/ppermute | solution.py:16
  641.8 53.5 %collective-permute-start.10 = (f32[2,128,768]{2,1,0:T(8,128)S(1)}, f32[2,128,768]{2,1,0:T(8,128)S(1)}, u32[]{:S(2)}, u32[]{:S(2)}) collective-permute-start(f32[2,128,768]{2,1,0:T(8,128)S(1)} %bitcast.147), channel_id=1, source_target_pairs={{0,1},{1,2},{2,3},{3,4},{4,5},{5,6},{6,7},{7,8},{8,9},{9,10},{10,1... | collective-permute-start | bytes 2359304 | tf_op jit(solution)/shard_map/ppermute | solution.py:16
  643.2 52.2 %collective-permute-start.9 = (f32[2,128,768]{2,1,0:T(8,128)S(1)}, f32[2,128,768]{2,1,0:T(8,128)S(1)}, u32[]{:S(2)}, u32[]{:S(2)}) collective-permute-start(f32[2,128,768]{2,1,0:T(8,128)S(1)} %bitcast.146), channel_id=1, source_target_pairs={{1,0},{2,1},{3,2},{4,3},{5,4},{6,5},{7,6},{8,7},{9,8},{10,9},{11,1... | collective-permute-start | bytes 2359304 | tf_op jit(solution)/shard_map/ppermute | solution.py:16
  (40 other events, 121.5 us)
Sparse Core Ops, SparseCore 0:
  629.2 221.4 all-reduce.2
where the time goes:
time: 877 us; the launch traced here: 868 us
  matrix products  354 us (40%)
  waiting for transfers between devices  209 us (24%)
  local copies, waits for them, and re-layouts  171 us (19%)
  other arithmetic  77.1 us (9%)
  starting transfers between devices  31.2 us (4%)
  between operations  14.8 us (2%)
  loops' own time  10.2 us (1%)
    psum x1, waiting for transfers between devices, per_device(): lax.psum((grad_query_part, grad_key_part, grad_value_part, grad_out_part)...  153 us
    dot_general x4, matrix products, frame_step(): jnp.einsum('hpk,phd->khd', dscores, queries, preferred_element_type=jnp.f...  109 us
    dot_general x4, matrix products, frame_step(): jnp.einsum('hpk,khd->phd', dscores, chosen_keys, preferred_element_type=j...  103 us
    ppermute x12, waiting for transfers between devices, shifted(): return lax.ppermute(block, axis, route)  55.9 us
    sub x4, matrix products, frame_step(): exponent = jnp.exp(scores - highest) * visible  38.1 us
    scatter-add x4, other arithmetic, per_frame(): running[1].at[local_tile].add(dvalues)  31.4 us
    scatter-add x4, other arithmetic, per_frame(): running[0].at[local_tile].add(dkeys)  31.2 us
    ppermute x12, starting transfers between devices, shifted(): return lax.ppermute(block, axis, route)  31.1 us
  transfers between devices with their start and end apart: 13, of which 3 were waited for; matrix products, arithmetic and copies ran while one was open for 3% of the time, Pallas kernels for 0%

commit v1 on v0

v1 whole, which is shorter than its diff:
```python
import functools
import math

import jax
import jax.numpy as jnp
from jax import lax
from jax.experimental import pallas as pl
from jax.experimental.pallas import tpu as pltpu
from jax.sharding import PartitionSpec as P

HEADS = 12
TILE = 128
REACH = 2
GROUPS = 3
SIZES = (2, 4, 6, 8)


def shifted(block, axis, distance):
    devices = range(lax.axis_size(axis))
    route = [(i - distance, i) for i in devices if i - distance in devices]
    return lax.ppermute(block, axis, route)


def normalize(row_block):
    centred = row_block.astype(jnp.float32)
    centred = centred - jnp.mean(centred, axis=-1, keepdims=True)
    inverse = lax.rsqrt(jnp.mean(centred * centred, axis=-1, keepdims=True) + 1e-05)
    normed_hat = centred * inverse
    return (normed_hat.astype(jnp.bfloat16), normed_hat, inverse)


def normalize_back(gradient, normed_hat, inverse):
    first = jnp.mean(gradient, axis=-1, keepdims=True)
    second = jnp.mean(gradient * normed_hat, axis=-1, keepdims=True)
    return inverse * (gradient - first - normed_hat * second)


def dot_nt(left, right):
    return lax.dot_general(left, right, (((1,), (1,)), ((), ())), preferred_element_type=jnp.float32)


def dot_nn(left, right):
    return jnp.dot(left, right, preferred_element_type=jnp.float32)


def per_head(reduced, low, high):
    rows = low.shape[0]
    return jnp.concatenate(
        [
            jnp.broadcast_to(reduced(low, axis=1, keepdims=True), (rows, TILE)),
            jnp.broadcast_to(reduced(high, axis=1, keepdims=True), (rows, TILE)),
        ],
        axis=1,
    )


def attention_kernel(
    tiles_ref,
    count_ref,
    fill_ref,
    query_ref,
    dcontext_ref,
    keys_ref,
    values_ref,
    context_ref,
    dquery_ref,
    dkeys_ref,
    dvalues_ref,
    pair_keys,
    pair_values,
    sum_keys,
    sum_values,
    query_pad,
    dcontext_pad,
    scores_scr,
    dattention_scr,
    low_scr,
    dscores_scr,
):
    frame = pl.program_id(1)
    patch = query_ref.shape[1]
    padded, width = query_pad.shape
    half = width // 2
    listed = tiles_ref.shape[1]
    window = pair_keys.shape[0]
    scale = 1.0 / math.sqrt(half)

    @pl.when(frame == 0)
    def _():
        first = lax.broadcasted_iota(jnp.int32, (TILE, width), 1) < half
        for tile in range(window):
            for source, target in ((keys_ref, pair_keys), (values_ref, pair_values)):
                block = source[tile * TILE : (tile + 1) * TILE, :]
                zero = jnp.zeros_like(block)
                target[tile, :TILE, :] = jnp.where(first, block, zero)
                target[tile, TILE:, :] = jnp.where(first, zero, block)
        sum_keys[...] = jnp.zeros_like(sum_keys)
        sum_values[...] = jnp.zeros_like(sum_values)
        for pad in (query_pad, dcontext_pad):
            pad[padded - 16 :, :] = jnp.zeros((16, width), pad.dtype)

    query_pad[:patch, :] = query_ref[0] * jnp.asarray(scale, query_ref.dtype)
    dcontext_pad[:patch, :] = dcontext_ref[0]
    count = count_ref[frame]

    def work(slots):
        query = query_pad[...]
        dcontext = dcontext_pad[...]
        query_t = query.T
        dcontext_t = dcontext.T
        lane = lax.rem(lax.broadcasted_iota(jnp.int32, (1, 2 * TILE), 1), TILE)
        places, biases = [], []
        for j in range(slots):
            place = tiles_ref[frame, j]
            seen = jnp.where(j < count, fill_ref[place], 0)
            places.append(place)
            biases.append(jnp.where(lane < seen, 0.0, -1e30))
        for j in range(slots):
            columns = slice(j * 2 * TILE, (j + 1) * 2 * TILE)
            scores_scr[:, columns] = dot_nt(query, pair_keys[places[j]]) + biases[j]
            dattention_scr[:, columns] = dot_nt(dcontext, pair_values[places[j]])
        for start in range(0, padded, 16):
            rows = slice(start, start + 16)
            scores = [scores_scr[rows, j * 2 * TILE : (j + 1) * 2 * TILE] for j in range(slots)]
            highest = functools.reduce(jnp.maximum, scores)
            highest = per_head(jnp.max, highest[:, :TILE], highest[:, TILE:])
            exponent = [jnp.exp(part - highest) for part in scores]
            total = functools.reduce(jnp.add, exponent)
            inverse = 1.0 / per_head(jnp.sum, total[:, :TILE], total[:, TILE:])
            attention = [part * inverse for part in exponent]
            dattention = [
                dattention_scr[rows, j * 2 * TILE : (j + 1) * 2 * TILE] for j in range(slots)
            ]
            weighed = functools.reduce(
                jnp.add, [a * b for a, b in zip(attention, dattention)]
            )
            weighed = per_head(jnp.sum, weighed[:, :TILE], weighed[:, TILE:])
            for j in range(slots):
                columns = slice(j * 2 * TILE, (j + 1) * 2 * TILE)
                low_scr[rows, columns] = attention[j].astype(jnp.bfloat16)
                dscores_scr[rows, columns] = (
                    attention[j] * (dattention[j] - weighed)
                ).astype(jnp.bfloat16)
        context = jnp.zeros((padded, width), jnp.float32)
        dquery = jnp.zeros((padded, width), jnp.float32)
        for j in range(slots):
            columns = slice(j * 2 * TILE, (j + 1) * 2 * TILE)
            low, dscores = low_scr[:, columns], dscores_scr[:, columns]
            context += dot_nn(low, pair_values[places[j]])
            dquery += dot_nn(dscores, pair_keys[places[j]])
            sum_keys[places[j]] += dot_nn(query_t, dscores)
            sum_values[places[j]] += dot_nn(dcontext_t, low)
        context_ref[0] = context[:patch].astype(context_ref.dtype)
        dquery_ref[0] = (dquery[:patch] * scale).astype(dquery_ref.dtype)

    least = 0
    for slots in sorted({min(size, listed) for size in SIZES} | {listed}):
        pl.when((count > least) & (count <= slots))(functools.partial(work, slots))
        least = slots

    @pl.when(frame == pl.num_programs(1) - 1)
    def _():
        for total, target in ((sum_keys, dkeys_ref), (sum_values, dvalues_ref)):
            for tile in range(window):
                columns = slice(tile * TILE, (tile + 1) * TILE)
                target[:half, columns] = total[tile, :half, :TILE].astype(target.dtype)
                target[half:, columns] = total[tile, half:, TILE:].astype(target.dtype)


def attend(local_block, count_block, fill_window, query, dcontext, key_window, value_window):
    frames, patch, width = query.shape
    slots = key_window.shape[0]
    window = slots // TILE
    listed = local_block.shape[1]
    pair = 2 * TILE // 2
    padded = -(-patch // 16) * 16
    frame_spec = pl.BlockSpec((1, patch, pair), lambda p, f, *_: (f, 0, p))
    window_spec = pl.BlockSpec((slots, pair), lambda p, f, *_: (0, p))
    sums_spec = pl.BlockSpec((pair, slots), lambda p, f, *_: (p, 0))
    work = frames * patch * width * listed * TILE
    return pl.pallas_call(
        attention_kernel,
        grid_spec=pltpu.PrefetchScalarGridSpec(
            num_scalar_prefetch=3,
            grid=(width // pair, frames),
            in_specs=[frame_spec, frame_spec, window_spec, window_spec],
            out_specs=[frame_spec, frame_spec, sums_spec, sums_spec],
            scratch_shapes=[
                pltpu.VMEM((window, 2 * TILE, pair), jnp.bfloat16),
                pltpu.VMEM((window, 2 * TILE, pair), jnp.bfloat16),
                pltpu.VMEM((window, pair, 2 * TILE), jnp.float32),
                pltpu.VMEM((window, pair, 2 * TILE), jnp.float32),
                pltpu.VMEM((padded, pair), jnp.bfloat16),
                pltpu.VMEM((padded, pair), jnp.bfloat16),
                pltpu.VMEM((padded, listed * 2 * TILE), jnp.float32),
                pltpu.VMEM((padded, listed * 2 * TILE), jnp.float32),
                pltpu.VMEM((padded, listed * 2 * TILE), jnp.bfloat16),
                pltpu.VMEM((padded, listed * 2 * TILE), jnp.bfloat16),
            ],
        ),
        out_shape=[
            jax.ShapeDtypeStruct(query.shape, jnp.bfloat16),
            jax.ShapeDtypeStruct(query.shape, jnp.bfloat16),
            jax.ShapeDtypeStruct((width, slots), jnp.bfloat16),
            jax.ShapeDtypeStruct((width, slots), jnp.bfloat16),
        ],
        compiler_params=pltpu.CompilerParams(vmem_limit_bytes=40 * 1024 * 1024),
        cost_estimate=pl.CostEstimate(
            flops=48 * work,
            bytes_accessed=8 * frames * patch * width + 8 * slots * width,
            transcendentals=work // 64,
        ),
        name="attend",
    )(local_block, count_block, fill_window, query, dcontext, key_window, value_window)


def per_device(
    video,
    audio,
    w_query,
    w_key,
    w_value,
    w_out,
    grad_output,
    intersection_tiles,
    intersection_count,
    tile_fill,
):
    tiles_dev = tile_fill.shape[0]
    window_tiles = (2 * REACH + 1) * tiles_dev
    frames = intersection_count.shape[0]
    features = video.shape[1]
    contract_rows = (((0,), (0,)), ((), ()))
    video_normed, video_hat, video_inverse = normalize(video)
    audio_normed, audio_hat, audio_inverse = normalize(audio)
    device_index = lax.axis_index(("frame", "audio"))
    normed_tiles = audio_normed.reshape(tiles_dev, TILE, features)
    normed_parts, fill_parts = ([], [])
    for offset in range(-REACH, REACH + 1):
        if offset == 0:
            received = (normed_tiles, tile_fill)
        else:
            received = shifted((normed_tiles, tile_fill), ("frame", "audio"), -offset)
        normed_parts.append(received[0])
        fill_parts.append(received[1])
    normed_window = jnp.concatenate(normed_parts, axis=0).reshape(-1, features)
    fill_window = jnp.concatenate(fill_parts, axis=0)
    local_block = jnp.clip(
        intersection_tiles - (device_index - REACH) * tiles_dev, 0, window_tiles - 1
    )
    group = features // GROUPS
    contexts, dqueries, dkeys, dvalues, sums = ([], [], [], [], [])
    for first in range(0, features, group):
        part = slice(first, first + group)
        query = dot_nn(video_normed, w_query[:, part]).astype(jnp.bfloat16)
        dcontext = dot_nt(grad_output, w_out[part]).astype(jnp.bfloat16)
        key_window = dot_nn(normed_window, w_key[:, part]).astype(jnp.bfloat16)
        value_window = dot_nn(normed_window, w_value[:, part]).astype(jnp.bfloat16)
        context, dquery, dkeys_t, dvalues_t = attend(
            local_block,
            intersection_count,
            fill_window,
            query.reshape(frames, -1, group),
            dcontext.reshape(frames, -1, group),
            key_window,
            value_window,
        )
        context = context.reshape(-1, group)
        dquery = dquery.reshape(-1, group)
        contexts.append(context)
        dqueries.append(dquery)
        dkeys.append(dkeys_t)
        dvalues.append(dvalues_t)
        window_rows = (((0,), (1,)), ((), ()))
        partial_sums = (
            lax.dot_general(
                video_normed, dquery, contract_rows, preferred_element_type=jnp.float32
            ),
            lax.dot_general(
                normed_window, dkeys_t, window_rows, preferred_element_type=jnp.float32
            ),
            lax.dot_general(
                normed_window, dvalues_t, window_rows, preferred_element_type=jnp.float32
            ),
            lax.dot_general(
                grad_output, context, contract_rows, preferred_element_type=jnp.float32
            ),
        )
        if sums:
            partial_sums, sums[-1] = lax.optimization_barrier((partial_sums, sums[-1]))
        sums.append(lax.psum(partial_sums, ("frame", "audio")))
    dkeys = jnp.concatenate(dkeys, axis=0)
    dvalues = jnp.concatenate(dvalues, axis=0)
    context = jnp.concatenate(contexts, axis=1)
    dquery = jnp.concatenate(dqueries, axis=1)
    rows_cols = (((0,), (1,)), ((), ()))
    dnormed_window = lax.dot_general(dkeys, w_key, rows_cols, preferred_element_type=jnp.float32)
    dnormed_window = dnormed_window + lax.dot_general(
        dvalues, w_value, rows_cols, preferred_element_type=jnp.float32
    )
    dnormed_window = dnormed_window.reshape(window_tiles, TILE, features)
    own_first = REACH * tiles_dev
    daudio_normed = dnormed_window[own_first : own_first + tiles_dev]
    for offset in range(-REACH, REACH + 1):
        if offset != 0:
            first_tile = (offset + REACH) * tiles_dev
            returned = shifted(
                dnormed_window[first_tile : first_tile + tiles_dev], ("frame", "audio"), offset
            )
            daudio_normed = daudio_normed + returned
    daudio_normed = daudio_normed.reshape(-1, features)
    grad_audio = normalize_back(daudio_normed, audio_hat, audio_inverse).astype(jnp.bfloat16)
    attended = dot_nn(context, w_out)
    output = (video.astype(jnp.float32) + attended).astype(jnp.bfloat16)
    dvideo_normed = dot_nt(dquery, w_query)
    grad_video = (
        grad_output.astype(jnp.float32) + normalize_back(dvideo_normed, video_hat, video_inverse)
    ).astype(jnp.bfloat16)
    grad_query, grad_key, grad_value = (
        jnp.concatenate([total[i] for total in sums], axis=1) for i in range(3)
    )
    grad_out = jnp.concatenate([total[3].T for total in sums], axis=0)
    return (output, grad_video, grad_audio, grad_query, grad_key, grad_value, grad_out)


def solution(mesh):
    in_specs = (
        P(("frame", "audio"), None),
        P(("frame", "audio"), None),
        P(),
        P(),
        P(),
        P(),
        P(("frame", "audio"), None),
        P(("frame", "audio"), None),
        P(("frame", "audio")),
        P(("frame", "audio")),
    )
    out_specs = (
        P(("frame", "audio"), None),
        P(("frame", "audio"), None),
        P(("frame", "audio"), None),
        P(),
        P(),
        P(),
        P(),
    )
    return jax.shard_map(
        per_device, mesh=mesh, in_specs=in_specs, out_specs=out_specs, check_vma=False
    )
```

time: 877 us -> 606 us (0.69)
  matrix products: 354 us -> 44.3 us
  waiting for transfers between devices: 209 us -> 429 us
  local copies, waits for them, and re-layouts: 171 us -> 19.9 us
  other arithmetic: 77.1 us -> 16.7 us
  Pallas kernels: 0 us -> 38.2 us
  loops' own time: 10.2 us -> 0 us
    dot_general x31 -> x25, matrix products: 313 us -> 36.9 us  [the longest x10 13.1 us: dot_nn(): return jnp.dot(left, right, preferred_element_type=jnp.float32)]
    psum x1 -> x3, waiting for transfers between devices: 153 us -> 418 us  [per_device(): sums.append(lax.psum(partial_sums, ('frame', 'audio')))]
    scatter-add x8 -> x0, other arithmetic: 62.6 us -> none  [the longest x4 31.4 us: per_frame(): running[1].at[local_tile].add(dvalues)]
    reshape x21 -> x12, local copies, waits for them, and re-layouts: 52.6 us -> 5.94 us  [the longest x3 2.23 us: per_device(): dcontext.reshape(frames, -1, group)]
    gather x20 -> x0, local copies, waits for them, and re-layouts: 46 us -> none  [the longest x8 21.9 us: frame_step(): chosen_keys = key_window[local_tile].reshape(-1, HEADS, head_size)]
    ppermute x12, waiting for transfers between devices: 55.9 us -> 10.8 us  [shifted(): return lax.ppermute(block, axis, route)]
    pallas_call x0 -> x3, Pallas kernels: none -> 38.2 us  [attend(): pl.pallas_call(attention_kernel, grid_spec=pltpu.PrefetchScalarGridSpec(n...]
    sub x4 -> x0, matrix products: 38.1 us -> none  [frame_step(): exponent = jnp.exp(scores - highest) * visible]
  transfers between devices with their start and end apart: 13 -> 15, of which waited for: 3 -> 6; matrix products, arithmetic and copies ran while one was open for 3% -> 7% of each run, Pallas kernels for 0% -> 0%
where the time goes in v1:
time: 606 us; the launch traced here: 601 us
  waiting for transfers between devices  429 us (71%)
  matrix products  44.3 us (7%)
  starting transfers between devices  38.5 us (6%)
  Pallas kernels  38.2 us (6%)
  local copies, waits for them, and re-layouts  19.9 us (3%)
  other arithmetic  16.7 us (3%)
  between operations  14.8 us (2%)
    psum x3, waiting for transfers between devices, per_device(): sums.append(lax.psum(partial_sums, ('frame', 'audio')))  418 us
    ppermute x12, starting transfers between devices, shifted(): return lax.ppermute(block, axis, route)  38.3 us
    pallas_call x3, Pallas kernels, attend(): pl.pallas_call(attention_kernel, grid_spec=pltpu.PrefetchScalarGridSpec(n...  38.2 us
    dot_general x10, matrix products, dot_nn(): return jnp.dot(left, right, preferred_element_type=jnp.float32)  13.1 us
  transfers between devices with their start and end apart: 15, of which 6 were waited for; matrix products, arithmetic and copies ran while one was open for 7% of the time, Pallas kernels for 0%

profile of v1, /device:TPU:0, one launch (start us, length us, event | category | flops | bytes accessed | tf_op | source)
XLA Modules:
  0.0 601.3 jit_solution(12398006289794927695)
XLA Ops:
  7.2 5.0 collective-permute-start
  17.3 4.6 collective-permute-start.4
  21.9 4.0 collective-permute-start.5
  42.8 3.0 collective-permute-done.3
  49.1 6.8 %collective-permute-done.7 = bf16[2,128,768]{2,1,0:T(8,128)(2,1)S(1)} collective-permute-done((bf16[2,128,768]{2,1,0:T(8,128)(2,1)S(1)}, bf16[2,128,768]{2,1,0:T(8,128)(2,1)S(1)}, u32[]{:S(2)}, u32[]{:S(2)}) %collective-permute-start.7) | collective-permute-done | bytes 393248 | tf_op jit(solution)/shard_map/ppermute | solution.py:21
  56.6 1.5 convolution_convert_fusion.3.keys_ref
  58.8 1.5 convolution_convert_fusion.2.values_ref
  63.3 12.5 %attend.5 = (bf16[4,196,256]{2,1,0:T(8,128)(2,1)S(1)}, bf16[4,196,256]{2,1,0:T(8,128)(2,1)S(1)}, bf16[256,1280]{1,0:T(8,128)(2,1)S(1)}, bf16[256,1280]{1,0:T(8,128)(2,1)S(1)}) custom-call(s32[4,8]{1,0:T(4,128)S(1)} %subtract_clamp_fusion.tiles_ref, s32[4]{0:T(128)S(1)} %copy-done, s32[10]{0:T(128)S(1)} %concatenate.30.fill_ref, ...), custom_call_target="tpu_custom_call" | custom-call | flops 9865003008 | bytes 4227072 | tf_op jit(solution)/shard_map/attend/pallas_call | solution.py:181
  80.6 12.7 %attend.3 = (bf16[4,196,256]{2,1,0:T(8,128)(2,1)S(1)}, bf16[4,196,256]{2,1,0:T(8,128)(2,1)S(1)}, bf16[256,1280]{1,0:T(8,128)(2,1)S(1)}, bf16[256,1280]{1,0:T(8,128)(2,1)S(1)}) custom-call(s32[4,8]{1,0:T(4,128)S(1)} %subtract_clamp_fusion.tiles_ref, s32[4]{0:T(128)S(1)} %copy-done, s32[10]{0:T(128)S(1)} %concatenate.30.fill_ref, ...), custom_call_target="tpu_custom_call" | custom-call | flops 9865003008 | bytes 4227072 | tf_op jit(solution)/shard_map/attend/pallas_call | solution.py:181
  97.6 3.3 fusion.67
  100.9 1.6 fusion.68
  102.5 12.9 %attend.4 = (bf16[4,196,256]{2,1,0:T(8,128)(2,1)S(1)}, bf16[4,196,256]{2,1,0:T(8,128)(2,1)S(1)}, bf16[256,1280]{1,0:T(8,128)(2,1)S(1)}, bf16[256,1280]{1,0:T(8,128)(2,1)S(1)}) custom-call(s32[4,8]{1,0:T(4,128)S(1)} %subtract_clamp_fusion.tiles_ref, s32[4]{0:T(128)S(1)} %copy-done, s32[10]{0:T(128)S(1)} %concatenate.30.fill_ref, ...), custom_call_target="tpu_custom_call" | custom-call | flops 9865003008 | bytes 4227072 | tf_op jit(solution)/shard_map/attend/pallas_call | solution.py:181
  115.5 1.8 fusion.12
  117.3 1.8 convolution_add_fusion
  119.1 2.0 fusion.62
  121.1 12.9 %collective-permute-start.11 = (f32[2,128,768]{2,1,0:T(8,128)}, f32[2,128,768]{2,1,0:T(8,128)}, u32[]{:S(2)}, u32[]{:S(2)}) collective-permute-start(f32[2,128,768]{2,1,0:T(8,128)} %bitcast.6), channel_id=1, source_target_pairs={{0,2},{1,3},{2,4},{3,5},{4,6},{5,7},{6,8},{7,9},{8,10},{9,11},{10,... | collective-permute-start | bytes 2359304 | tf_op jit(solution)/shard_map/ppermute | solution.py:21
  134.0 2.4 collective-permute-start.10
  143.1 2.8 fusion.69
  146.1 3.0 fusion.63
  149.1 1.5 convolution_bitcast_fusion.2
  150.6 1.7 fusion.70
  152.3 1.6 fusion.64
  153.9 1.6 fusion.65
  155.5 143.1 %all-reduce.11.cloned.1.call-done = (f32[768,256]{1,0:T(8,128)}, f32[768,256]{1,0:T(8,128)}, f32[768,256]{1,0:T(8,128)}, f32[768,256]{0,1:T(8,128)}) async-done(((f32[768,256]{1,0:T(8,128)}, f32[768,256]{1,0:T(8,128)}, f32[768,256]{1,0:T(8,128)}, f32[768,256]{0,1:T(8,128)}), (f32[768,256]{1,0:T(8,128)}, f32[768,256]{1,0:T(8,128)}, f32[768,256]{1,0:T(8,128)}, ...) | async-done | bytes 3145744 | tf_op jit(solution)/shard_map/psum | solution.py:291
  300.3 1.6 fusion.71
  303.9 1.9 fusion.9
  305.8 138.1 %all-reduce.9.cloned.1.call-done = (f32[768,256]{1,0:T(8,128)}, f32[768,256]{1,0:T(8,128)}, f32[768,256]{1,0:T(8,128)}, f32[768,256]{0,1:T(8,128)}) async-done(((f32[768,256]{1,0:T(8,128)}, f32[768,256]{1,0:T(8,128)}, f32[768,256]{1,0:T(8,128)}, f32[768,256]{0,1:T(8,128)}), (f32[768,256]{1,0:T(8,128)}, f32[768,256]{1,0:T(8,128)}, f32[768,256]{1,0:T(8,128)}, ...) | async-done | bytes 3145744 | tf_op jit(solution)/shard_map/psum | solution.py:291
  443.9 3.5 fusion.11
  447.4 2.2 fusion.61
  451.0 137.0 %all-reduce.7.cloned.1.call-done = (f32[768,256]{1,0:T(8,128)}, f32[768,256]{1,0:T(8,128)}, f32[768,256]{1,0:T(8,128)}, f32[256,768]{1,0:T(8,128)}) async-done(((f32[768,256]{1,0:T(8,128)}, f32[768,256]{1,0:T(8,128)}, f32[768,256]{1,0:T(8,128)}, f32[256,768]{1,0:T(8,128)}), (f32[768,256]{1,0:T(8,128)}, f32[768,256]{1,0:T(8,128)}, f32[768,256]{1,0:T(8,128)}, ...) | async-done | bytes 3145744 | tf_op jit(solution)/shard_map/psum | solution.py:291
  588.1 4.0 pad_maximum_fusion
  592.1 2.5 pad_maximum_fusion.2
  (193 shorter events, 50.2 us)
Async XLA Ops:
  7.2 20.0 %copy-start.20 = (bf16[784,768]{1,0:T(8,128)(2,1)S(1)}, bf16[784,768]{1,0:T(8,128)(2,1)}, u32[]{:S(2)}) copy-start(bf16[784,768]{1,0:T(8,128)(2,1)} %param.10) | copy-start | bytes 3612676
  7.2 291.4 %all-reduce.11.cloned.1.call-start = ((), (), s32[]{:S(2)}) async-start(), calls=%async_computation.2 | async-start | bytes 6291456 | tf_op jit(solution)/shard_map/psum | solution.py:291
  7.2 30.4 %collective-permute-start = (s32[2]{0:T(128)}, s32[2]{0:T(128)S(1)}, u32[]{:S(2)}, u32[]{:S(2)}) collective-permute-start(s32[2]{0:T(128)} %param.19), channel_id=1, source_target_pairs={{0,2},{1,3},{2,4},{3,5},{4,6},{5,7},{6,8},{7,9},{8,10},{9,11},{10,... | collective-permute-start | bytes 32 | tf_op jit(solution)/shard_map/ppermute | solution.py:21
  12.2 26.7 %collective-permute-start.1 = (s32[2]{0:T(128)}, s32[2]{0:T(128)S(1)}, u32[]{:S(2)}, u32[]{:S(2)}) collective-permute-start(s32[2]{0:T(128)} %param.19), channel_id=1, source_target_pairs={{0,1},{1,2},{2,3},{3,4},{4,5},{5,6},{6,7},{7,8},{8,9},{9,10},{10,1... | collective-permute-start | bytes 32 | tf_op jit(solution)/shard_map/ppermute | solution.py:21
  17.3 28.6 %collective-permute-start.4 = (bf16[2,128,768]{2,1,0:T(8,128)(2,1)S(1)}, bf16[2,128,768]{2,1,0:T(8,128)(2,1)}, u32[]{:S(2)}, u32[]{:S(2)}) collective-permute-start(bf16[2,128,768]{2,1,0:T(8,128)(2,1)S(1)} %bitcast.65), channel_id=1, source_target_pairs={{0,2},{1,3},{2,4},{3,5},{4,6},{5,7},{6,8},{7,9},{8,10},{9,11},{10,... | collective-permute-start | bytes 1179656 | tf_op jit(solution)/shard_map/ppermute | solution.py:21
  21.9 25.1 %collective-permute-start.5 = (bf16[2,128,768]{2,1,0:T(8,128)(2,1)S(1)}, bf16[2,128,768]{2,1,0:T(8,128)(2,1)}, u32[]{:S(2)}, u32[]{:S(2)}) collective-permute-start(bf16[2,128,768]{2,1,0:T(8,128)(2,1)S(1)} %bitcast.66), channel_id=1, source_target_pairs={{0,1},{1,2},{2,3},{3,4},{4,5},{5,6},{6,7},{7,8},{8,9},{9,10},{10,1... | collective-permute-start | bytes 1179656 | tf_op jit(solution)/shard_map/ppermute | solution.py:21
  25.9 22.2 %collective-permute-start.6 = (bf16[2,128,768]{2,1,0:T(8,128)(2,1)S(1)}, bf16[2,128,768]{2,1,0:T(8,128)(2,1)}, u32[]{:S(2)}, u32[]{:S(2)}) collective-permute-start(bf16[2,128,768]{2,1,0:T(8,128)(2,1)S(1)} %bitcast.67), channel_id=1, source_target_pairs={{1,0},{2,1},{3,2},{4,3},{5,4},{6,5},{7,6},{8,7},{9,8},{10,9},{11,1... | collective-permute-start | bytes 1179656 | tf_op jit(solution)/shard_map/ppermute | solution.py:21
  37.6 3.7 collective-permute-start.2
  38.9 6.8 %collective-permute-start.3 = (s32[2]{0:T(128)S(1)}, s32[2]{0:T(128)S(1)}, u32[]{:S(2)}, u32[]{:S(2)}) collective-permute-start(s32[2]{0:T(128)S(1)} %copy-done.53), channel_id=1, source_target_pairs={{2,0},{3,1},{4,2},{5,3},{6,4},{7,5},{8,6},{9,7},{10,8},{11,9},{12,... | collective-permute-start | bytes 32 | tf_op jit(solution)/shard_map/ppermute | solution.py:21
  41.3 14.5 %collective-permute-start.7 = (bf16[2,128,768]{2,1,0:T(8,128)(2,1)S(1)}, bf16[2,128,768]{2,1,0:T(8,128)(2,1)S(1)}, u32[]{:S(2)}, u32[]{:S(2)}) collective-permute-start(bf16[2,128,768]{2,1,0:T(8,128)(2,1)S(1)} %bitcast.68), channel_id=1, source_target_pairs={{2,0},{3,1},{4,2},{5,3},{6,4},{7,5},{8,6},{9,7},{10,8},{11,9},{12,... | collective-permute-start | bytes 1179656 | tf_op jit(solution)/shard_map/ppermute | solution.py:21
  45.8 10.0 %copy-start.54 = (bf16[768,768]{1,0:T(8,128)(2,1)S(1)}, bf16[768,768]{1,0:T(8,128)(2,1)}, u32[]{:S(2)}) copy-start(bf16[768,768]{1,0:T(8,128)(2,1)} %param.13) | copy-start | bytes 3538948
  102.5 13.0 %copy-start.4 = (bf16[256,1280]{1,0:T(8,128)(2,1)S(1)}, bf16[256,1280]{1,0:T(8,128)(2,1)}, u32[]{:S(2)}) copy-start(bf16[256,1280]{1,0:T(8,128)(2,1)} %copy-done.3) | copy-start | bytes 1966084
  102.5 13.0 %copy-start.11 = (bf16[256,1280]{1,0:T(8,128)(2,1)S(1)}, bf16[256,1280]{1,0:T(8,128)(2,1)}, u32[]{:S(2)}) copy-start(bf16[256,1280]{1,0:T(8,128)(2,1)} %copy-done.9) | copy-start | bytes 1966084
  102.5 13.0 %copy-start.55 = (bf16[768,768]{1,0:T(8,128)(2,1)S(1)}, bf16[768,768]{1,0:T(8,128)(2,1)}, u32[]{:S(2)}) copy-start(bf16[768,768]{1,0:T(8,128)(2,1)} %param.13) | copy-start | bytes 3538948
  119.1 19.9 %copy-start.30 = (bf16[784,768]{1,0:T(8,128)(2,1)S(1)}, bf16[784,768]{1,0:T(8,128)(2,1)}, u32[]{:S(2)}) copy-start(bf16[784,768]{1,0:T(8,128)(2,1)} %copy-done.29) | copy-start | bytes 3612676
  119.1 19.9 %copy-start.43 = (bf16[784,256]{1,0:T(8,128)(2,1)S(1)}, bf16[784,256]{1,0:T(8,128)(2,1)}, u32[]{:S(2)}) copy-start(bf16[784,256]{1,0:T(8,128)(2,1)} %reshape.122) | copy-start | bytes 1204228
  121.1 19.5 %copy-start.17 = (bf16[784,768]{1,0:T(8,128)(2,1)S(1)}, bf16[784,768]{1,0:T(8,128)(2,1)}, u32[]{:S(2)}) copy-start(bf16[784,768]{1,0:T(8,128)(2,1)} %param.16) | copy-start | bytes 3612676
  121.1 19.5 %copy-start.25 = (bf16[784,256]{1,0:T(8,128)(2,1)S(1)}, bf16[784,256]{1,0:T(8,128)(2,1)}, u32[]{:S(2)}) copy-start(bf16[784,256]{1,0:T(8,128)(2,1)} %reshape.115) | copy-start | bytes 1204228
  121.1 326.3 %collective-permute-start.11 = (f32[2,128,768]{2,1,0:T(8,128)}, f32[2,128,768]{2,1,0:T(8,128)}, u32[]{:S(2)}, u32[]{:S(2)}) collective-permute-start(f32[2,128,768]{2,1,0:T(8,128)} %bitcast.6), channel_id=1, source_target_pairs={{0,2},{1,3},{2,4},{3,5},{4,6},{5,7},{6,8},{7,9},{8,10},{9,11},{10,... | collective-permute-start | bytes 2359304 | tf_op jit(solution)/shard_map/ppermute | solution.py:21
  134.0 313.4 %collective-permute-start.10 = (f32[2,128,768]{2,1,0:T(8,128)}, f32[2,128,768]{2,1,0:T(8,128)}, u32[]{:S(2)}, u32[]{:S(2)}) collective-permute-start(f32[2,128,768]{2,1,0:T(8,128)} %bitcast.5), channel_id=1, source_target_pairs={{0,1},{1,2},{2,3},{3,4},{4,5},{5,6},{6,7},{7,8},{8,9},{9,10},{10,1... | collective-permute-start | bytes 2359304 | tf_op jit(solution)/shard_map/ppermute | solution.py:21
  136.4 310.9 %collective-permute-start.9 = (f32[2,128,768]{2,1,0:T(8,128)}, f32[2,128,768]{2,1,0:T(8,128)}, u32[]{:S(2)}, u32[]{:S(2)}) collective-permute-start(f32[2,128,768]{2,1,0:T(8,128)} %bitcast.4), channel_id=1, source_target_pairs={{1,0},{2,1},{3,2},{4,3},{5,4},{6,5},{7,6},{8,7},{9,8},{10,9},{11,1... | collective-permute-start | bytes 2359304 | tf_op jit(solution)/shard_map/ppermute | solution.py:21
  137.7 309.7 %collective-permute-start.8 = (f32[2,128,768]{2,1,0:T(8,128)}, f32[2,128,768]{2,1,0:T(8,128)}, u32[]{:S(2)}, u32[]{:S(2)}) collective-permute-start(f32[2,128,768]{2,1,0:T(8,128)} %bitcast.3), channel_id=1, source_target_pairs={{2,0},{3,1},{4,2},{5,3},{6,4},{7,5},{8,6},{9,7},{10,8},{11,9},{12,... | collective-permute-start | bytes 2359304 | tf_op jit(solution)/shard_map/ppermute | solution.py:21
  142.1 301.7 %all-reduce.9.cloned.1.call-start = ((), (), s32[]{:S(2)}) async-start(), calls=%async_computation.1 | async-start | bytes 6291456 | tf_op jit(solution)/shard_map/psum | solution.py:291
  155.5 143.2 %copy-start.19 = (bf16[784,768]{1,0:T(8,128)(2,1)S(1)}, bf16[784,768]{1,0:T(8,128)(2,1)}, u32[]{:S(2)}) copy-start(bf16[784,768]{1,0:T(8,128)(2,1)} %param.16) | copy-start | bytes 3612676
  155.5 143.2 %copy-start.24 = (bf16[784,256]{1,0:T(8,128)(2,1)S(1)}, bf16[784,256]{1,0:T(8,128)(2,1)}, u32[]{:S(2)}) copy-start(bf16[784,256]{1,0:T(8,128)(2,1)} %reshape.121) | copy-start | bytes 1204228
  298.6 289.4 %all-reduce.7.cloned.1.call-start = ((), (), s32[]{:S(2)}) async-start(), calls=%async_computation | async-start | bytes 6291456 | tf_op jit(solution)/shard_map/psum | solution.py:291
  305.8 138.1 %copy-start.26 = (bf16[784,256]{1,0:T(8,128)(2,1)S(1)}, bf16[784,256]{1,0:T(8,128)(2,1)}, u32[]{:S(2)}) copy-start(bf16[784,256]{1,0:T(8,128)(2,1)} %reshape.115) | copy-start | bytes 1204228
  305.8 138.1 %copy-start.28 = (bf16[784,256]{1,0:T(8,128)(2,1)S(1)}, bf16[784,256]{1,0:T(8,128)(2,1)}, u32[]{:S(2)}) copy-start(bf16[784,256]{1,0:T(8,128)(2,1)} %copy-done.27) | copy-start | bytes 1204228
  447.4 140.6 %copy-start.38 = (f32[768,256]{1,0:T(8,128)S(1)}, f32[768,256]{1,0:T(8,128)}, u32[]{:S(2)}) copy-start(f32[768,256]{1,0:T(8,128)} %get-tuple-element.55) | copy-start | bytes 2359300
  449.7 138.3 %copy-start.33 = (f32[768,256]{1,0:T(8,128)S(1)}, f32[768,256]{1,0:T(8,128)}, u32[]{:S(2)}) copy-start(f32[768,256]{1,0:T(8,128)} %get-tuple-element.47) | copy-start | bytes 2359300
  449.7 138.3 %copy-start.34 = (f32[768,256]{1,0:T(8,128)S(1)}, f32[768,256]{1,0:T(8,128)}, u32[]{:S(2)}) copy-start(f32[768,256]{1,0:T(8,128)} %get-tuple-element.54) | copy-start | bytes 2359300
  449.7 138.3 %copy-start.37 = (f32[768,256]{1,0:T(8,128)S(1)}, f32[768,256]{1,0:T(8,128)}, u32[]{:S(2)}) copy-start(f32[768,256]{1,0:T(8,128)} %get-tuple-element.52) | copy-start | bytes 2359300
  (44 other events, 108.9 us)
Sparse Core Ops, SparseCore 0:
  142.2 156.3 all-reduce.10
  306.2 137.6 all-reduce.8
  450.4 137.5 all-reduce.6
